TPU v7x, 32 devices: a whole 2x2x4 slice. The times are simulated.
32 devices in a mesh: section: 4 (over x, core), seq: 2 (over y), tp: 4 (over z).
Axes of the slice: x: 2, y: 2, z: 4, core: 2. Of those that a mesh axis runs over, the one named last changes fastest.
Arguments:
- frames: bfloat16 [4, 2048, 1536], P('section', ('seq', 'tp')), may hold values from -64 to 64
- pointwise_in: bfloat16 [1536, 3072], P(None, 'tp'), may hold values from -0.15625 to 0.15625
- depth_kernel: float32 [31, 1536], P(None, 'tp'), may hold values from -1 to 1
- norm_scale: float32 [1536], P('tp'), may hold values from 0.5 to 2
- norm_shift: float32 [1536], P('tp'), may hold values from -3 to 3
- pointwise_out: bfloat16 [1536, 1536], P('tp'), may hold values from -0.21875 to 0.21875
- adapter_weight: bfloat16 [6144, 8192], P(('section', 'seq'), 'tp'), may hold values from -0.078125 to 0.078125
Outputs:
- arrival: bfloat16 [4, 512, 8192], P('section', 'seq', 'tp')
All inputs are finite; a program needn't handle non-finite values.
Results may differ from a plain program's by a relative error of at most 0.01.
Values may be sent and summed in bfloat16 or wider, within the bound.
A program may use at most 128 MiB of HBM per device.

v0:
```python
import jax
import jax.numpy as jnp
from jax import lax
from jax.sharding import PartitionSpec as P

STACK = 4


norm_eps = 1e-05


def with_halo(cells, sides, width):
    for axis, dim in sides:
        count = lax.axis_size(axis)
        ends = count - 1
        head = lax.slice_in_dim(cells, 0, width, axis=dim)
        tail = lax.slice_in_dim(cells, cells.shape[dim] - width, cells.shape[dim], axis=dim)
        cells = jnp.concatenate(
            [
                lax.ppermute(tail, axis, [(i, (i + 1) % count) for i in range(ends)]),
                cells,
                lax.ppermute(head, axis, [((i + 1) % count, i) for i in range(ends)]),
            ],
            axis=dim,
        )
    return cells


def shifted(x, axis, by):
    length = lax.axis_size(axis)
    return lax.ppermute(x, axis, [(i, (i + by) % length) for i in range(length)])


def layer_norm_rows(signal):
    centred = signal - jnp.mean(signal, axis=-1, keepdims=True)
    variance = jnp.mean(centred * centred, axis=-1, keepdims=True)
    return (centred * lax.rsqrt(variance + norm_eps)).astype(jnp.bfloat16)


def add_rows(inputs, weight_rows):
    return jnp.dot(inputs, weight_rows, preferred_element_type=jnp.float32)


def per_device(
    frames, pointwise_in, depth_kernel, norm_scale, norm_shift, pointwise_out, adapter_weight
):
    gathered = lax.all_gather(frames, "tp", axis=1, tiled=True)
    signal = gathered[0].astype(jnp.float32)
    frame_count = signal.shape[0]
    channels = signal.shape[1]
    local_channels = pointwise_in.shape[1] // 2
    normed = layer_norm_rows(signal)
    projected = jnp.dot(normed, pointwise_in, preferred_element_type=jnp.float32)
    gated = (projected[:, :local_channels] * jax.nn.sigmoid(projected[:, local_channels:])).astype(
        jnp.bfloat16
    )
    taps = depth_kernel.shape[0]
    half_width = (taps - 1) // 2
    padded = with_halo(gated, (("seq", 0),), half_width)
    filtered = jnp.zeros((frame_count, local_channels), jnp.float32)
    for offset in range(taps):
        filtered = filtered + padded[offset : offset + frame_count] * depth_kernel[offset]
    activated = jax.nn.silu(filtered * norm_scale + norm_shift).astype(jnp.bfloat16)
    partial_value = jnp.dot(activated, pointwise_out, preferred_element_type=jnp.float32)
    token_count = frame_count // STACK
    share = lax.psum_scatter(
        partial_value.astype(jnp.bfloat16), "tp", scatter_dimension=1, tiled=True
    ).astype(jnp.float32)
    own_start = lax.axis_index("tp") * local_channels
    own_signal = lax.dynamic_slice_in_dim(signal, own_start, local_channels, 1)
    encoded = (own_signal + share).astype(jnp.bfloat16)
    grouped = lax.all_gather(
        encoded.reshape(token_count, STACK, local_channels), "tp", axis=2, tiled=True
    )
    stacked = grouped.reshape(token_count, STACK * channels)
    bridged = add_rows(
        stacked, lax.all_gather(adapter_weight, ("section", "seq"), axis=0, tiled=True)
    )
    arrival = shifted(bridged.astype(jnp.bfloat16)[None], "section", 1)
    return arrival


def solution(mesh):
    placed = (
        P("section", ("seq", "tp"), None),
        P(None, "tp"),
        P(None, "tp"),
        P("tp"),
        P("tp"),
        P("tp", None),
        P(("section", "seq"), "tp"),
    )
    return jax.shard_map(
        per_device, mesh=mesh, in_specs=placed, out_specs=P("section", "seq", "tp"), check_vma=False
    )
```

profile of v0, /device:TPU:0, one launch (start us, length us, event | category | flops | bytes accessed | tf_op | source)
XLA Modules:
  0.0 398.1 jit_solution(7111941026976875069)
XLA Ops:
  6.5 0.7 all-gather.4.cloned.1.call-update
  7.3 0.0 reduce-scatter.4.cloned.1.call-start
  7.3 1.2 slice_reduce_fusion.30
  8.5 66.6 %all-gather.4.cloned.1.call-done = bf16[1,1024,1536]{2,1,0:T(8,128)(2,1)} async-done(((bf16[1,256,1536]{2,1,0:T(8,128)(2,1)}), bf16[1,1024,1536]{2,1,0:T(8,128)(2,1)}) %all-gather.4.cloned.1.call-update) | async-done | bytes 3145744 | tf_op jit(solution)/shard_map/all_gather | solution.py:47
  75.2 2.5 convert_reduce_fusion
  77.7 0.3 copy-done.1
  78.0 1.0 multiply_reduce_fusion
  79.0 2.7 fusion
  81.7 0.4 fusion.9
  82.2 3.4 collective-permute-start
  85.6 1.3 collective-permute-start.1
  86.9 1.0 slice_reduce_fusion.29
  87.9 3.2 collective-permute-done.1
  91.2 14.6 %convolution_convert_fusion = bf16[1024,1536]{1,0:T(8,128)(2,1)} fusion(bf16[384,1536]{1,0:T(8,128)(2,1)S(1)} %copy-done.2, bf16[1024,384]{1,0:T(8,128)(2,1)S(1)} %fusion.9, bf16[15,384]{1,0:T(8,128)(2,1)S(1)} %collective-permute-done.1, bf16[15,384]{1,0:T(8,128)(2,1)S(1)} %collective-permute-done, f32[384]{0:T(512)S(1)} %copy-done.3, ...), kind=kOutput, calls=%fused_computation.32 | convolution fusion | flops 1283850240 | bytes 5185536 | tf_op jit(solution)/shard_map/dot_general | solution.py:64
  105.8 4.6 %copy.8 = bf16[1024,1536]{0,1:T(8,128)(2,1)} copy(bf16[1024,1536]{1,0:T(8,128)(2,1)} %convolution_convert_fusion) | data formatting | bytes 6291456
  110.4 0.0 reduce-scatter.4.cloned.1.call-update
  110.4 0.0 all-gather.6.cloned.1.call-start
  110.5 5.4 %convert_element_type.120 = f32[1,1024,1536]{2,1,0:T(8,128)} convert(bf16[1,1024,1536]{2,1,0:T(8,128)(2,1)} %all-gather.4.cloned.1.call-done) | non-fusion elementwise | flops 1572864 | bytes 9437184 | tf_op jit(solution)/shard_map/convert_element_type | solution.py:48
  115.9 52.6 %reduce-scatter.4.cloned.1.call-done = bf16[384,1024]{1,0:T(8,128)(2,1)} async-done(((bf16[1536,1024]{1,0:T(8,128)(2,1)}), bf16[384,1024]{1,0:T(8,128)(2,1)}) %reduce-scatter.4.cloned.1.call-update) | async-done | bytes 786448
  168.6 1.5 copy.9
  170.1 2.5 fusion.8
  172.5 2.4 reshape.22
  174.9 0.0 all-gather.6.cloned.1.call-update
  174.9 0.2 all-gather.8.cloned.1.call-start
  175.2 0.3 all-gather.8.cloned.1.call-update
  175.5 63.0 %all-gather.6.cloned.1.call-done = bf16[256,4,1536]{2,1,0:T(4,128)(2,1)} async-done(((bf16[256,4,384]{2,1,0:T(4,128)(2,1)}), bf16[256,4,1536]{2,1,0:T(4,128)(2,1)}) %all-gather.6.cloned.1.call-update) | async-done | bytes 3145744 | tf_op jit(solution)/shard_map/all_gather | solution.py:72
  238.5 4.4 %copy.10 = bf16[32,8,4,1536]{3,1,2,0:T(8,128)(2,1)} copy(bf16[32,8,4,1536]{3,2,1,0:T(4,128)(2,1)} %bitcast.22) | data formatting | bytes 6291456
  243.0 120.8 %all-gather.8.cloned.1.call-done = bf16[6144,2048]{1,0:T(8,128)(2,1)} async-done(((bf16[768,2048]{1,0:T(8,128)(2,1)}), bf16[6144,2048]{1,0:T(8,128)(2,1)}) %all-gather.8.cloned.1.call-update) | async-done | bytes 25165840 | tf_op jit(solution)/shard_map/all_gather | solution.py:77
  363.8 12.5 %fusion.3 = bf16[1,256,2048]{2,1,0:T(8,128)(2,1)S(1)} fusion(bf16[256,6144]{1,0:T(8,128)(2,1)} %bitcast.23, bf16[6144,2048]{1,0:T(8,128)(2,1)} %all-gather.8.cloned.1.call-done), kind=kOutput, calls=%fused_computation.37 | convolution fusion | flops 6442975232 | bytes 29360128 | tf_op jit(solution)/shard_map/dot_general | solution.py:41
  376.3 0.3 collective-permute-start.2
  376.6 14.0 %collective-permute-done.2 = bf16[1,256,2048]{2,1,0:T(8,128)(2,1)S(1)} collective-permute-done((bf16[1,256,2048]{2,1,0:T(8,128)(2,1)S(1)}, bf16[1,256,2048]{2,1,0:T(8,128)(2,1)S(1)}, u32[]{:S(2)}, u32[]{:S(2)}) %collective-permute-start.2) | collective-permute-done | bytes 1048608 | tf_op jit(solution)/shard_map/ppermute | solution.py:31
  390.6 1.0 copy.12
  (14 shorter events, 0.1 us)
Async XLA Ops:
  6.5 72.4 %copy-start = (bf16[1536,768]{1,0:T(8,128)(2,1)S(1)}, bf16[1536,768]{1,0:T(8,128)(2,1)}, u32[]{:S(2)}) copy-start(bf16[1536,768]{1,0:T(8,128)(2,1)} %param.8) | copy-start | bytes 7077892
  6.5 68.6 %all-gather.4.cloned.1.call-start = ((), (), s32[]{:S(2)}) async-start(), calls=%async_computation.1 | async-start | bytes 3932160 | tf_op jit(solution)/shard_map/all_gather | solution.py:47
  7.3 161.3 %reduce-scatter.4.cloned.1.call-start = ((), (), s32[]{:S(2)}) async-start(), calls=%async_computation.4 | async-start | bytes 3932160
  75.2 2.8 copy-start.1
  81.7 9.5 %copy-start.2 = (bf16[384,1536]{1,0:T(8,128)(2,1)S(1)}, bf16[384,1536]{1,0:T(8,128)(2,1)}, u32[]{:S(2)}) copy-start(bf16[384,1536]{1,0:T(8,128)(2,1)} %param.12) | copy-start | bytes 3538948
  81.7 9.5 %copy-start.3 = (f32[384]{0:T(512)S(1)}, f32[384]{0:T(512)}, u32[]{:S(2)}) copy-start(f32[384]{0:T(512)} %param.11) | copy-start | bytes 4612
  81.7 9.4 %copy-start.4 = (f32[384]{0:T(512)S(1)}, f32[384]{0:T(512)}, u32[]{:S(2)}) copy-start(f32[384]{0:T(512)} %param.10) | copy-start | bytes 4612
  82.2 5.7 %collective-permute-start = (bf16[15,384]{1,0:T(8,128)(2,1)S(1)}, bf16[15,384]{1,0:T(8,128)(2,1)S(1)}, u32[]{:S(2)}, u32[]{:S(2)}) collective-permute-start(bf16[15,384]{1,0:T(8,128)(2,1)S(1)} %get-tuple-element.36), channel_id=1, source_target_pairs={{0,4},{1,5},{2,6},{3,7},{8,12},{9,13},{10,14},{11,15},{16,20},{17,... | collective-permute-start | bytes 34568 | tf_op jit(solution)/shard_map/ppermute | solution.py:20
  85.6 5.6 %collective-permute-start.1 = (bf16[15,384]{1,0:T(8,128)(2,1)S(1)}, bf16[15,384]{1,0:T(8,128)(2,1)S(1)}, u32[]{:S(2)}, u32[]{:S(2)}) collective-permute-start(bf16[15,384]{1,0:T(8,128)(2,1)S(1)} %get-tuple-element.37), channel_id=1, source_target_pairs={{4,0},{5,1},{6,2},{7,3},{12,8},{13,9},{14,10},{15,11},{20,16},{21,... | collective-permute-start | bytes 34568 | tf_op jit(solution)/shard_map/ppermute | solution.py:22
  110.4 128.1 %all-gather.6.cloned.1.call-start = ((), (), s32[]{:S(2)}) async-start(), calls=%async_computation.2 | async-start | bytes 3932160 | tf_op jit(solution)/shard_map/all_gather | solution.py:72
  174.9 188.9 %all-gather.8.cloned.1.call-start = ((), (), s32[]{:S(2)}) async-start(), calls=%async_computation.3 | async-start | bytes 28311552 | tf_op jit(solution)/shard_map/all_gather | solution.py:77
  376.3 14.3 %collective-permute-start.2 = (bf16[1,256,2048]{2,1,0:T(8,128)(2,1)S(1)}, bf16[1,256,2048]{2,1,0:T(8,128)(2,1)S(1)}, u32[]{:S(2)}, u32[]{:S(2)}) collective-permute-start(bf16[1,256,2048]{2,1,0:T(8,128)(2,1)S(1)} %fusion.3), channel_id=1, source_target_pairs={{0,8},{8,16},{16,24},{24,0},{1,9},{9,17},{17,25},{25,1},{2,10},{10... | collective-permute-start | bytes 3145736 | tf_op jit(solution)/shard_map/ppermute | solution.py:31
Sparse Core Ops, SparseCore 0:
  8.9 66.1 all-gather.3
  110.6 57.9 reduce-scatter.3
  175.1 63.4 all-gather.5
  240.3 123.4 all-gather.7
where the time goes:
time: 399 us; the launch traced here: 398 us
  waiting for transfers between devices  321 us (80%)
  matrix products  29.8 us (7%)
  local copies, waits for them, and re-layouts  16.5 us (4%)
  between operations  13.2 us (3%)
  other arithmetic  11.8 us (3%)
  starting transfers between devices  5.29 us (1%)
    all_gather x1, waiting for transfers between devices, per_device(): lax.all_gather(adapter_weight, ('section', 'seq'), axis=0, tiled=True)  121 us
    all_gather x1, waiting for transfers between devices, per_device(): gathered = lax.all_gather(frames, 'tp', axis=1, tiled=True)  66.6 us
    all_gather x1, waiting for transfers between devices, per_device(): lax.all_gather(encoded.reshape(token_count, STACK, local_channels), 'tp',...  63 us
    unnamed x5, waiting for transfers between devices  53.7 us
    dot_general x1, matrix products, per_device(): jnp.dot(activated, pointwise_out, preferred_element_type=jnp.float32)  14.6 us
    ppermute x1, waiting for transfers between devices, shifted(): lax.ppermute(x, axis, [(i, (i + by) % length) for i in range(length)])  14 us
    dot_general x1, matrix products, add_rows(): return jnp.dot(inputs, weight_rows, preferred_element_type=jnp.float32)  12.5 us
    unnamed x14, local copies, waits for them, and re-layouts  11.9 us
  transfers between devices with their start and end apart: 7, of which 6 were waited for; matrix products, arithmetic and copies ran while one was open for 3% of the time, Pallas kernels for 0%

commit v1 on v0

v1 whole, which is shorter than its diff:
```python
import jax
import jax.numpy as jnp
from jax import lax
from jax.sharding import PartitionSpec as P

STACK = 4
HALO = 16

norm_eps = 1e-05


def layer_norm_rows(signal):
    centred = signal - jnp.mean(signal, axis=-1, keepdims=True)
    variance = jnp.mean(centred * centred, axis=-1, keepdims=True)
    return (centred * lax.rsqrt(variance + norm_eps)).astype(jnp.bfloat16)


def own_piece(array, count, index):
    rows = array.shape[0] // count
    return lax.dynamic_slice_in_dim(array, index * rows, rows, 0)


def per_device(
    frames, pointwise_in, depth_kernel, norm_scale, norm_shift, pointwise_out, adapter_weight
):
    tp = lax.axis_size("tp")
    copies = lax.axis_size("section") * lax.axis_size("seq")
    copy_index = lax.axis_index("section") * lax.axis_size("seq") + lax.axis_index("seq")
    everywhere = ("tp", "section", "seq")
    rows = frames.shape[1]
    channels = frames.shape[2]
    block = channels // tp
    taps = depth_kernel.shape[0]
    half_width = (taps - 1) // 2

    own = frames[0]
    count = lax.axis_size("seq") * tp
    before = lax.ppermute(own[rows - HALO :], ("seq", "tp"), [(i, i + 1) for i in range(count - 1)])
    after = lax.ppermute(own[:HALO], ("seq", "tp"), [(i + 1, i) for i in range(count - 1)])

    small = jnp.concatenate([depth_kernel, norm_scale[None], norm_shift[None]], axis=0)
    small = lax.all_gather(small, "tp", axis=0)
    small = jnp.swapaxes(small, 0, 1).reshape(taps + 2, channels)
    win = lax.all_gather(own_piece(pointwise_in, copies, copy_index), everywhere, axis=0, tiled=True)
    win = win.reshape(tp, channels, 2 * block)
    wout = lax.all_gather(own_piece(pointwise_out, copies, copy_index), everywhere, axis=0, tiled=True)

    extended = jnp.concatenate([before, own, after], axis=0).astype(jnp.float32)
    normed = layer_norm_rows(extended)
    gated = []
    for b in range(tp):
        projected = jnp.dot(normed, win[b], preferred_element_type=jnp.float32)
        gated.append(
            (projected[:, :block] * jax.nn.sigmoid(projected[:, block:])).astype(jnp.bfloat16)
        )
    padded = jnp.concatenate(gated, axis=1)
    filtered = jnp.zeros((rows, channels), jnp.float32)
    first = HALO - half_width
    for offset in range(taps):
        filtered = filtered + padded[first + offset : first + offset + rows] * small[offset]
    activated = jax.nn.silu(filtered * small[taps] + small[taps + 1]).astype(jnp.bfloat16)
    mixed = jnp.dot(activated, wout, preferred_element_type=jnp.float32)
    encoded = (own.astype(jnp.float32) + mixed).astype(jnp.bfloat16)
    stacked = encoded.reshape(rows // STACK, STACK * channels)
    stacked = lax.all_gather(stacked, "tp", axis=0, tiled=True)
    weight = lax.all_gather(adapter_weight, ("section", "seq"), axis=0, tiled=True)
    bridged = jnp.dot(stacked, weight, preferred_element_type=jnp.float32).astype(jnp.bfloat16)
    sections = lax.axis_size("section")
    return lax.ppermute(
        bridged[None], "section", [(i, (i + 1) % sections) for i in range(sections)]
    )


def solution(mesh):
    placed = (
        P("section", ("seq", "tp"), None),
        P(None, "tp"),
        P(None, "tp"),
        P("tp"),
        P("tp"),
        P("tp", None),
        P(("section", "seq"), "tp"),
    )
    return jax.shard_map(
        per_device, mesh=mesh, in_specs=placed, out_specs=P("section", "seq", "tp"), check_vma=False
    )
```

time: 399 us -> 414 us (1.038)
  blocking collectives: 0 us -> 16.6 us
  matrix products: 29.8 us -> 44.5 us
  waiting for transfers between devices: 321 us -> 309 us
  other arithmetic: 11.8 us -> 2.13 us
  local copies, waits for them, and re-layouts: 16.5 us -> 20.9 us
    unnamed x5 -> x4, waiting for transfers between devices: 53.7 us -> 0.39 us
    all_gather x2 -> x3, waiting for transfers between devices: 130 us -> 169 us  [the longest x1 61.9 us: per_device(): stacked = lax.all_gather(stacked, 'tp', axis=0, tiled=True)]
    all_gather x0 -> x1, blocking collectives: none -> 16.6 us  [per_device(): small = lax.all_gather(small, 'tp', axis=0)]
    dot_general x3 -> x6, matrix products: 29.8 us -> 44.5 us  [the longest x1 26.6 us: per_device(): mixed = jnp.dot(activated, wout, preferred_element_type=jnp.float32)]
    mul x0 -> x32, local copies, waits for them, and re-layouts: none -> 8.58 us  [the longest x31 8.57 us: per_device(): padded[first + offset:first + offset + rows] * small[offset]]
    convert_element_type x3 -> x2, other arithmetic: 8.32 us -> 0.49 us  [per_device(): (projected[:, :block] * jax.nn.sigmoid(projected[:, block:])).astype(jnp....]
    unnamed x14 -> x29, local copies, waits for them, and re-layouts: 11.9 us -> 4.34 us
    all_gather x1, waiting for transfers between devices: 121 us -> 126 us  [per_device(): lax.all_gather(adapter_weight, ('section', 'seq'), axis=0, tiled=True)]
  transfers between devices with their start and end apart: 7 -> 7, of which waited for: 6 -> 5; matrix products, arithmetic and copies ran while one was open for 3% -> 5% of each run, Pallas kernels for 0% -> 0%
where the time goes in v1:
time: 414 us; the launch traced here: 413 us
  waiting for transfers between devices  309 us (75%)
  matrix products  44.5 us (11%)
  local copies, waits for them, and re-layouts  20.9 us (5%)
  blocking collectives  16.6 us (4%)
  between operations  13.5 us (3%)
  starting transfers between devices  6.86 us (2%)
    all_gather x1, waiting for transfers between devices, per_device(): lax.all_gather(adapter_weight, ('section', 'seq'), axis=0, tiled=True)  126 us
    all_gather x1, waiting for transfers between devices, per_device(): stacked = lax.all_gather(stacked, 'tp', axis=0, tiled=True)  61.9 us
    all_gather x1, waiting for transfers between devices, per_device(): lax.all_gather(own_piece(pointwise_out, copies, copy_index), everywhere,...  56.4 us
    all_gather x1, waiting for transfers between devices, per_device(): lax.all_gather(own_piece(pointwise_in, copies, copy_index), everywhere, a...  50.6 us
    dot_general x1, matrix products, per_device(): mixed = jnp.dot(activated, wout, preferred_element_type=jnp.float32)  26.6 us
    all_gather x1, blocking collectives, per_device(): small = lax.all_gather(small, 'tp', axis=0)  16.6 us
    ppermute x1, waiting for transfers between devices, per_device(): lax.ppermute(bridged[None], 'section', [(i, (i + 1) % sections) for i in...  14 us
    dot_general x1, matrix products, per_device(): jnp.dot(stacked, weight, preferred_element_type=jnp.float32)  12.5 us
  transfers between devices with their start and end apart: 7, of which 5 were waited for; matrix products, arithmetic and copies ran while one was open for 5% of the time, Pallas kernels for 0%

profile of v1, /device:TPU:0, one launch (start us, length us, event | category | flops | bytes accessed | tf_op | source)
XLA Modules:
  0.0 413.4 jit_solution(9066692902649333548)
XLA Ops:
  6.6 1.7 copy-done
  8.3 0.7 constant_dynamic-slice_fusion.1
  9.1 1.6 constant_dynamic-slice_fusion
  10.7 0.8 slice_bitcast_fusion.1
  11.6 4.9 %collective-permute-start = (bf16[16,1536]{1,0:T(8,128)(2,1)S(1)}, bf16[16,1536]{1,0:T(8,128)(2,1)S(1)}, u32[]{:S(2)}, u32[]{:S(2)}) collective-permute-start(bf16[16,1536]{1,0:T(8,128)(2,1)S(1)} %get-tuple-element.38), channel_id=1, source_target_pairs={{0,1},{1,2},{2,3},{3,4},{4,5},{5,6},{6,7},{8,9},{9,10},{10,11},{11... | collective-permute-start | bytes 147464 | tf_op jit(solution)/shard_map/ppermute | solution.py:38
  16.5 1.3 collective-permute-start.1
  17.9 16.6 %all-gather.1 = f32[4,33,384]{2,1,0:T(8,128)S(1)} all-gather(f32[1,33,384]{2,1,0:T(8,128)S(1)} %maximum_bitcast_fusion), channel_id=2, replica_groups=mesh['section'=4,'seq'=2,'tp'=4] {'tp'}, dimensions={0}, use_global_device_ids=true | all-gather | bytes 253440 | tf_op jit(solution)/shard_map/all_gather | solution.py:42
  34.4 0.9 slice_reduce_fusion.32
  35.6 1.3 add.177
  36.9 1.3 mul.365
  38.2 1.3 mul.410
  39.5 1.3 mul.413
  40.8 1.3 mul.416
  42.1 1.3 mul.419
  43.3 1.3 mul.422
  44.6 0.6 mul.425
  45.8 0.4 fusion.12
  46.2 50.6 %all-gather.7.cloned.1.call-done = bf16[6144,768]{1,0:T(8,128)(2,1)} async-done(((bf16[192,768]{1,0:T(8,128)(2,1)}), bf16[6144,768]{1,0:T(8,128)(2,1)}) %all-gather.7.cloned.1.call-update) | async-done | bytes 9437200 | tf_op jit(solution)/shard_map/all_gather | solution.py:44
  96.8 2.7 fusion.6
  99.5 1.7 copy-done.13
  101.2 0.9 fusion.8
  102.3 0.9 fusion.2
  103.3 0.9 fusion.4
  104.5 1.0 pad_maximum_fusion.1
  105.5 56.4 %all-gather.9.cloned.1.call-done = bf16[1536,1536]{1,0:T(8,128)(2,1)} async-done(((bf16[48,1536]{1,0:T(8,128)(2,1)}), bf16[1536,1536]{1,0:T(8,128)(2,1)}) %all-gather.9.cloned.1.call-update) | async-done | bytes 4718608 | tf_op jit(solution)/shard_map/all_gather | solution.py:46
  162.0 26.6 %fusion = bf16[256,1536]{1,0:T(8,128)(2,1)} fusion(bf16[1536,1536]{1,0:T(8,128)(2,1)} %all-gather.9.cloned.1.call-done, bf16[288,1536]{1,0:T(8,128)(2,1)} %pad_maximum_fusion.1, f32[1536]{0:T(1024)S(1)} %copy-done.3, f32[1536]{0:T(1024)S(1)} %mul.458, f32[1536]{0:T(1024)S(1)} %mul.455, f32[1536]{0:T(1024)S(1)} %mul.452, f32[1536]{0:T(1024)S(1)} %mul.449, ...), kind=kOutput, calls=%fused_computation.2 | convolution fusion | flops 1248067584 | bytes 30873600 | tf_op jit(solution)/shard_map/dot_general | solution.py:62
  188.6 2.3 reshape.93
  191.5 61.9 %all-gather.11.cloned.1.call-done = bf16[256,6144]{1,0:T(8,128)(2,1)} async-done(((bf16[64,6144]{1,0:T(8,128)(2,1)}), bf16[256,6144]{1,0:T(8,128)(2,1)}) %all-gather.11.cloned.1.call-update) | async-done | bytes 3145744 | tf_op jit(solution)/shard_map/all_gather | solution.py:65
  253.4 125.7 %all-gather.13.cloned.1.call-done = bf16[6144,2048]{1,0:T(8,128)(2,1)} async-done(((bf16[768,2048]{1,0:T(8,128)(2,1)}), bf16[6144,2048]{1,0:T(8,128)(2,1)}) %all-gather.13.cloned.1.call-update) | async-done | bytes 25165840 | tf_op jit(solution)/shard_map/all_gather | solution.py:66
  379.2 12.5 %fusion.1 = bf16[1,256,2048]{2,1,0:T(8,128)(2,1)S(1)} fusion(bf16[256,6144]{1,0:T(8,128)(2,1)} %all-gather.11.cloned.1.call-done, bf16[6144,2048]{1,0:T(8,128)(2,1)} %all-gather.13.cloned.1.call-done), kind=kOutput, calls=%fused_computation.3 | convolution fusion | flops 6442975232 | bytes 29360128 | tf_op jit(solution)/shard_map/dot_general | solution.py:67
  392.0 14.0 %collective-permute-done.2 = bf16[1,256,2048]{2,1,0:T(8,128)(2,1)S(1)} collective-permute-done((bf16[1,256,2048]{2,1,0:T(8,128)(2,1)S(1)}, bf16[1,256,2048]{2,1,0:T(8,128)(2,1)S(1)}, u32[]{:S(2)}, u32[]{:S(2)}) %collective-permute-start.2) | collective-permute-done | bytes 1048608 | tf_op jit(solution)/shard_map/ppermute | solution.py:69
  405.9 1.0 copy.9
  (71 shorter events, 2.3 us)
Async XLA Ops:
  6.5 1.7 copy-start
  6.5 39.0 %copy-start.1 = (bf16[1,256,1536]{2,1,0:T(8,128)(2,1)S(1)}, bf16[1,256,1536]{2,1,0:T(8,128)(2,1)}, u32[]{:S(2)}) copy-start(bf16[1,256,1536]{2,1,0:T(8,128)(2,1)} %param.7) | copy-start | bytes 2359300
  6.5 11.3 %copy-start.11 = (f32[384]{0:T(512)S(1)}, f32[384]{0:T(512)}, u32[]{:S(2)}) copy-start(f32[384]{0:T(512)} %param.10) | copy-start | bytes 4612
  6.5 11.3 %copy-start.12 = (f32[384]{0:T(512)S(1)}, f32[384]{0:T(512)}, u32[]{:S(2)}) copy-start(f32[384]{0:T(512)} %param.11) | copy-start | bytes 4612
  6.5 11.3 %copy-start.2 = (f32[31,384]{1,0:T(8,128)S(1)}, f32[31,384]{1,0:T(8,128)}, u32[]{:S(2)}) copy-start(f32[31,384]{1,0:T(8,128)} %param.9) | copy-start | bytes 142852
  6.5 90.2 %all-gather.7.cloned.1.call-start = ((), (), s32[]{:S(2)}) async-start(), calls=%async_computation | async-start | bytes 9732096 | tf_op jit(solution)/shard_map/all_gather | solution.py:44
  9.0 152.9 %all-gather.9.cloned.1.call-start = ((), (), s32[]{:S(2)}) async-start(), calls=%async_computation.1 | async-start | bytes 4866048 | tf_op jit(solution)/shard_map/all_gather | solution.py:46
  10.7 242.8 %all-gather.11.cloned.1.call-start = ((), (), s32[]{:S(2)}) async-start(), calls=%async_computation.2 | async-start | bytes 3932160 | tf_op jit(solution)/shard_map/all_gather | solution.py:65
  11.6 34.0 %collective-permute-start = (bf16[16,1536]{1,0:T(8,128)(2,1)S(1)}, bf16[16,1536]{1,0:T(8,128)(2,1)S(1)}, u32[]{:S(2)}, u32[]{:S(2)}) collective-permute-start(bf16[16,1536]{1,0:T(8,128)(2,1)S(1)} %get-tuple-element.38), channel_id=1, source_target_pairs={{0,1},{1,2},{2,3},{3,4},{4,5},{5,6},{6,7},{8,9},{9,10},{10,11},{11... | collective-permute-start | bytes 147464 | tf_op jit(solution)/shard_map/ppermute | solution.py:38
  16.5 29.1 %collective-permute-start.1 = (bf16[16,1536]{1,0:T(8,128)(2,1)S(1)}, bf16[16,1536]{1,0:T(8,128)(2,1)S(1)}, u32[]{:S(2)}, u32[]{:S(2)}) collective-permute-start(bf16[16,1536]{1,0:T(8,128)(2,1)S(1)} %get-tuple-element.39), channel_id=1, source_target_pairs={{1,0},{2,1},{3,2},{4,3},{5,4},{6,5},{7,6},{9,8},{10,9},{11,10},{12... | collective-permute-start | bytes 147464 | tf_op jit(solution)/shard_map/ppermute | solution.py:39
  96.8 4.4 %copy-start.13 = (bf16[6144,768]{1,0:T(8,128)(2,1)S(1)}, bf16[6144,768]{1,0:T(8,128)(2,1)}, u32[]{:S(2)}) copy-start(bf16[6144,768]{1,0:T(8,128)(2,1)} %all-gather.7.cloned.1.call-done) | copy-start | bytes 28311556
  104.2 57.8 %copy-start.3 = (f32[1536]{0:T(1024)S(1)}, f32[1536]{0:T(1024)}, u32[]{:S(2)}) copy-start(f32[1536]{0:T(1024)} %add.177) | copy-start | bytes 18436
  104.2 57.8 %copy-start.4 = (f32[1536]{0:T(1024)S(1)}, f32[1536]{0:T(1024)}, u32[]{:S(2)}) copy-start(f32[1536]{0:T(1024)} %mul.365) | copy-start | bytes 18436
  104.2 57.8 %copy-start.5 = (f32[1536]{0:T(1024)S(1)}, f32[1536]{0:T(1024)}, u32[]{:S(2)}) copy-start(f32[1536]{0:T(1024)} %mul.410) | copy-start | bytes 18436
  104.2 57.8 %copy-start.6 = (f32[1536]{0:T(1024)S(1)}, f32[1536]{0:T(1024)}, u32[]{:S(2)}) copy-start(f32[1536]{0:T(1024)} %mul.413) | copy-start | bytes 18436
  104.2 57.7 %copy-start.7 = (f32[1536]{0:T(1024)S(1)}, f32[1536]{0:T(1024)}, u32[]{:S(2)}) copy-start(f32[1536]{0:T(1024)} %mul.416) | copy-start | bytes 18436
  104.2 57.7 %copy-start.8 = (f32[1536]{0:T(1024)S(1)}, f32[1536]{0:T(1024)}, u32[]{:S(2)}) copy-start(f32[1536]{0:T(1024)} %mul.419) | copy-start | bytes 18436
  104.2 57.7 %copy-start.9 = (f32[1536]{0:T(1024)S(1)}, f32[1536]{0:T(1024)}, u32[]{:S(2)}) copy-start(f32[1536]{0:T(1024)} %mul.422) | copy-start | bytes 18436
  104.3 57.7 %copy-start.10 = (f32[1536]{0:T(1024)S(1)}, f32[1536]{0:T(1024)}, u32[]{:S(2)}) copy-start(f32[1536]{0:T(1024)} %mul.425) | copy-start | bytes 18436
  191.0 188.2 %all-gather.13.cloned.1.call-start = ((), (), s32[]{:S(2)}) async-start(), calls=%async_computation.3 | async-start | bytes 28311552 | tf_op jit(solution)/shard_map/all_gather | solution.py:66
  391.7 14.3 %collective-permute-start.2 = (bf16[1,256,2048]{2,1,0:T(8,128)(2,1)S(1)}, bf16[1,256,2048]{2,1,0:T(8,128)(2,1)S(1)}, u32[]{:S(2)}, u32[]{:S(2)}) collective-permute-start(bf16[1,256,2048]{2,1,0:T(8,128)(2,1)S(1)} %fusion.1), channel_id=1, source_target_pairs={{0,8},{8,16},{16,24},{24,0},{1,9},{9,17},{17,25},{25,1},{2,10},{10... | collective-permute-start | bytes 3145736 | tf_op jit(solution)/shard_map/ppermute | solution.py:69
Sparse Core Ops, SparseCore 0:
  10.3 86.4 all-gather.6
  99.7 62.2 all-gather.8
  191.1 62.2 all-gather.10
  255.2 123.9 all-gather.12

commit v2 on v1

--- a/solution.py
+++ b/solution.py
@@ -1,10 +1,15 @@
+import functools
+
 import jax
 import jax.numpy as jnp
 from jax import lax
+from jax.experimental import pallas as pl
+from jax.experimental.pallas import tpu as pltpu
 from jax.sharding import PartitionSpec as P
 
 STACK = 4
 HALO = 16
+MESH = pl.DeviceIdType.MESH
 
 norm_eps = 1e-05
 
@@ -18,6 +23,210 @@
 def own_piece(array, count, index):
     rows = array.shape[0] // count
     return lax.dynamic_slice_in_dim(array, index * rows, rows, 0)
+
+
+def adapter_kernel(
+    axes, tile, enc_ref, w_ref, out_ref,
+    wbuf, tok, psend, precv,
+    w_sem, w_send, w_recv, a_send, right_send, left_send, tok_recv, p_send, p_recv,
+):
+    sections, seqs, depth = axes
+    section, seq, layer = lax.axis_index("section"), lax.axis_index("seq"), lax.axis_index("tp")
+    core, side = section % 2, section // 2
+    sides = sections // 2
+    after = (section + 1) % sections
+    steps = [(i, j) for i in range(sides) for j in range(seqs)]
+    steps = steps[1:][::-1] + steps[:1]
+    groups = len(steps)
+    tiles = out_ref.shape[1] // tile
+
+    barrier = pltpu.get_barrier_semaphore()
+    for i in range(sections):
+        for j in range(seqs):
+            if i + j > 0:
+                pl.semaphore_signal(
+                    barrier, inc=1, device_id_type=MESH,
+                    device_id=((section + i) % sections, (seq + j) % seqs, layer),
+                )
+
+    @pl.when(layer > 0)
+    def _():
+        pl.semaphore_signal(
+            barrier, inc=1, device_id=(section, seq, layer - 1), device_id_type=MESH
+        )
+
+    @pl.when(layer < depth - 1)
+    def _():
+        pl.semaphore_signal(
+            barrier, inc=1, device_id=(section, seq, layer + 1), device_id_type=MESH
+        )
+
+    neighbours = (layer + depth - 1) // depth + (2 * depth - 2 - layer) // depth
+    pl.semaphore_wait(barrier, sections * seqs - 1 + neighbours)
+
+    def remote(src, dst, send, recv, target):
+        return pltpu.make_async_remote_copy(
+            src_ref=src, dst_ref=dst, send_sem=send, recv_sem=recv,
+            device_id=target, device_id_type=MESH,
+        )
+
+    own_w = pltpu.make_async_copy(w_ref, wbuf.at[core], w_sem)
+    own_w.start()
+
+    def a_copy(g):
+        i, j = steps[g]
+        to_side = (after // 2 - i + sides) % sides
+        to_seq = (seq - j + seqs) % seqs
+        return remote(
+            enc_ref.at[pl.ds(2 * to_side, 2), to_seq], tok.at[g, layer],
+            a_send.at[g], tok_recv.at[g, layer], (2 * to_side + after % 2, to_seq, layer),
+        )
+
+    for g in range(groups):
+        a_copy(g).start()
+    other_w = remote(
+        w_ref, wbuf.at[core], w_send, w_recv, (section + 1 - 2 * core, seq, layer)
+    )
+    other_w.start()
+
+    def pass_right(g, origin):
+        return remote(
+            tok.at[g, origin], tok.at[g, origin], right_send.at[g, origin],
+            tok_recv.at[g, origin], (section, seq, layer + 1),
+        )
+
+    def pass_left(g, origin):
+        return remote(
+            tok.at[g, origin], tok.at[g, origin], left_send.at[g, origin],
+            tok_recv.at[g, origin], (section, seq, layer - 1),
+        )
+
+    def arrived(g, origin):
+        remote(
+            tok.at[g, origin], tok.at[g, origin], a_send.at[g],
+            tok_recv.at[g, origin], (section + 1 - 2 * core, seq, layer),
+        ).wait_recv()
+
+    def pass_both(g):
+        arrived(g, layer)
+
+        @pl.when(layer < depth - 1)
+        def _():
+            pass_right(g, layer).start()
+
+        @pl.when(layer > 0)
+        def _():
+            pass_left(g, layer).start()
+
+    def p_copy(g, t):
+        i, j = steps[g]
+        columns = pl.ds(pl.multiple_of(t * tile, tile), tile)
+        to_side = (side + i) % sides
+        return remote(
+            psend.at[g, :, columns], precv.at[g, :, columns],
+            p_send.at[g, t], p_recv.at[g, t], (2 * to_side + core, (seq + j) % seqs, layer),
+        )
+
+    def product(g, columns):
+        shape = (depth * tok.shape[3], tok.shape[4])
+        total = jnp.dot(
+            tok[g, :, 0].reshape(shape), wbuf[0, :, columns], preferred_element_type=jnp.float32
+        )
+        return total + jnp.dot(
+            tok[g, :, 1].reshape(shape), wbuf[1, :, columns], preferred_element_type=jnp.float32
+        )
+
+    pass_both(0)
+    pass_both(1)
+    for g in range(groups):
+        for hop in range(1, depth):
+
+            @pl.when(layer - hop >= 0)
+            def _():
+                arrived(g, layer - hop)
+
+                @pl.when(layer < depth - 1)
+                def _():
+                    pass_right(g, layer - hop).start()
+
+            @pl.when(layer + hop < depth)
+            def _():
+                arrived(g, layer + hop)
+
+                @pl.when(layer > 0)
+                def _():
+                    pass_left(g, layer + hop).start()
+
+        if g + 2 < groups:
+            pass_both(g + 2)
+        if g == 0:
+            own_w.wait()
+            other_w.wait()
+
+        if g < groups - 1:
+
+            @pl.loop(0, tiles)
+            def _(t):
+                columns = pl.ds(pl.multiple_of(t * tile, tile), tile)
+                psend[g, :, columns] = product(g, columns).astype(jnp.bfloat16)
+                p_copy(g, t).start()
+
+        else:
+
+            @pl.loop(0, tiles)
+            def _(t):
+                columns = pl.ds(pl.multiple_of(t * tile, tile), tile)
+                total = product(g, columns)
+                for k in range(groups - 1):
+                    p_copy(k, t).wait_recv()
+                    total = total + precv[k, :, columns].astype(jnp.float32)
+                out_ref[:, columns] = total.astype(jnp.bfloat16)
+
+    for g in range(groups):
+        a_copy(g).wait_send()
+        for origin in range(depth):
+
+            @pl.when((layer < depth - 1) & (origin <= layer))
+            def _():
+                pass_right(g, origin).wait_send()
+
+            @pl.when((layer > 0) & (origin >= layer))
+            def _():
+                pass_left(g, origin).wait_send()
+
+        if g < groups - 1:
+
+            @pl.loop(0, tiles)
+            def _(t):
+                p_copy(g, t).wait_send()
+
+
+def adapter(enc, weight, tokens):
+    axes = (lax.axis_size("section"), lax.axis_size("seq"), lax.axis_size("tp"))
+    sections, seqs, depth = axes
+    groups = sections // 2 * seqs
+    few, width = enc.shape[2:]
+    columns = weight.shape[1]
+    tile = 512
+    tiles = columns // tile
+    dma = pltpu.SemaphoreType.DMA
+    return pl.pallas_call(
+        functools.partial(adapter_kernel, axes, tile),
+        out_shape=jax.ShapeDtypeStruct((tokens, columns), jnp.bfloat16),
+        in_specs=[pl.BlockSpec(memory_space=pltpu.VMEM), pl.BlockSpec(memory_space=pl.ANY)],
+        out_specs=pl.BlockSpec(memory_space=pltpu.VMEM),
+        scratch_shapes=[
+            pltpu.VMEM((2, width, columns), jnp.bfloat16),
+            pltpu.VMEM((groups, depth, 2, few, width), jnp.bfloat16),
+            pltpu.VMEM((groups - 1, tokens, columns), jnp.bfloat16),
+            pltpu.VMEM((groups - 1, tokens, columns), jnp.bfloat16),
+            dma, dma, dma, dma((groups,)), dma((groups, depth)), dma((groups, depth)),
+            dma((groups, depth)), dma((groups - 1, tiles)), dma((groups - 1, tiles)),
+        ],
+        compiler_params=pltpu.CompilerParams(
+            collective_id=0, has_side_effects=True, vmem_limit_bytes=48 * 2**20
+        ),
+    )(enc, weight)
 
 
 def per_device(
@@ -61,14 +270,10 @@
     activated = jax.nn.silu(filtered * small[taps] + small[taps + 1]).astype(jnp.bfloat16)
     mixed = jnp.dot(activated, wout, preferred_element_type=jnp.float32)
     encoded = (own.astype(jnp.float32) + mixed).astype(jnp.bfloat16)
-    stacked = encoded.reshape(rows // STACK, STACK * channels)
-    stacked = lax.all_gather(stacked, "tp", axis=0, tiled=True)
-    weight = lax.all_gather(adapter_weight, ("section", "seq"), axis=0, tiled=True)
-    bridged = jnp.dot(stacked, weight, preferred_element_type=jnp.float32).astype(jnp.bfloat16)
-    sections = lax.axis_size("section")
-    return lax.ppermute(
-        bridged[None], "section", [(i, (i + 1) % sections) for i in range(sections)]
-    )
+    seqs = lax.axis_size("seq")
+    enc = encoded.reshape(rows // STACK, STACK, seqs, channels // seqs)
+    enc = jnp.transpose(enc, (1, 2, 0, 3))
+    return adapter(enc, adapter_weight, rows // STACK * tp)[None]
 
 
 def solution(mesh):

time: 414 us -> 280 us (0.68)
  waiting for transfers between devices: 309 us -> 106 us
  Pallas kernels: 0 us -> 80.2 us
  matrix products: 44.5 us -> 30.5 us
    all_gather x2 -> x0, waiting for transfers between devices: 188 us -> none  [the longest x1 126 us: per_device(): lax.all_gather(adapter_weight, ('section', 'seq'), axis=0, tiled=True)]
    pallas_call x0 -> x1, Pallas kernels: none -> 80.2 us  [adapter(): pl.pallas_call(functools.partial(adapter_kernel, axes, tile), out_shape=j...]
    ppermute x1 -> x0, waiting for transfers between devices: 14 us -> none  [per_device(): lax.ppermute(bridged[None], 'section', [(i, (i + 1) % sections) for i in...]
    dot_general x1 -> x0, matrix products: 12.5 us -> none  [per_device(): jnp.dot(stacked, weight, preferred_element_type=jnp.float32)]
  transfers between devices with their start and end apart: 7 -> 4, of which waited for: 5 -> 2; matrix products, arithmetic and copies ran while one was open for 5% -> 8% of each run, Pallas kernels for 0% -> 0%
where the time goes in v2:
time: 280 us; the launch traced here: 279 us
  waiting for transfers between devices  106 us (38%)
  Pallas kernels  80.2 us (29%)
  matrix products  30.5 us (11%)
  local copies, waits for them, and re-layouts  23.5 us (8%)
  blocking collectives  16.7 us (6%)
  between operations  13.7 us (5%)
  starting transfers between devices  6.28 us (2%)
    pallas_call x1, Pallas kernels, adapter(): pl.pallas_call(functools.partial(adapter_kernel, axes, tile), out_shape=j...  80.2 us
    all_gather x1, waiting for transfers between devices, per_device(): lax.all_gather(own_piece(pointwise_out, copies, copy_index), everywhere,...  56.4 us
    all_gather x1, waiting for transfers between devices, per_device(): lax.all_gather(own_piece(pointwise_in, copies, copy_index), everywhere, a...  49.7 us
    dot_general x1, matrix products, per_device(): mixed = jnp.dot(activated, wout, preferred_element_type=jnp.float32)  25 us
    all_gather x1, blocking collectives, per_device(): small = lax.all_gather(small, 'tp', axis=0)  16.7 us
    mul x31, local copies, waits for them, and re-layouts, per_device(): padded[first + offset:first + offset + rows] * small[offset]  8.57 us
    unnamed x29, local copies, waits for them, and re-layouts  6.22 us
  transfers between devices with their start and end apart: 4, of which 2 were waited for; matrix products, arithmetic and copies ran while one was open for 8% of the time, Pallas kernels for 0%

profile of v2, /device:TPU:0, one launch (start us, length us, event | category | flops | bytes accessed | tf_op | source)
XLA Modules:
  0.0 279.3 jit_solution(8441232184995262550)
XLA Ops:
  6.6 1.6 copy-done
  8.2 0.7 constant_dynamic-slice_fusion.1
  9.1 1.6 constant_dynamic-slice_fusion
  10.7 0.8 slice_bitcast_fusion.1
  11.5 4.9 %collective-permute-start = (bf16[16,1536]{1,0:T(8,128)(2,1)S(1)}, bf16[16,1536]{1,0:T(8,128)(2,1)S(1)}, u32[]{:S(2)}, u32[]{:S(2)}) collective-permute-start(bf16[16,1536]{1,0:T(8,128)(2,1)S(1)} %get-tuple-element.38), channel_id=1, source_target_pairs={{0,1},{1,2},{2,3},{3,4},{4,5},{5,6},{6,7},{8,9},{9,10},{10,11},{11... | collective-permute-start | bytes 147464 | tf_op jit(solution)/shard_map/ppermute | solution.py:247
  16.4 1.3 collective-permute-start.1
  17.7 0.7 broadcast_in_dim.11
  18.4 16.7 %all-gather.1 = f32[4,33,384]{2,1,0:T(8,128)S(1)} all-gather(f32[1,33,384]{2,1,0:T(8,128)S(1)} %maximum_bitcast_fusion), channel_id=2, replica_groups=mesh['section'=4,'seq'=2,'tp'=4] {'tp'}, dimensions={0}, use_global_device_ids=true | all-gather | bytes 253440 | tf_op jit(solution)/shard_map/all_gather | solution.py:251
  35.1 0.9 slice_reduce_fusion.32
  36.3 1.3 add.177
  37.6 1.3 mul.365
  38.9 1.3 mul.410
  40.2 1.3 mul.413
  41.5 1.3 mul.416
  42.8 1.3 mul.419
  44.0 1.3 mul.422
  45.4 0.6 mul.425
  46.5 0.4 fusion.11
  46.9 49.7 %all-gather.5.cloned.1.call-done = bf16[6144,768]{1,0:T(8,128)(2,1)} async-done(((bf16[192,768]{1,0:T(8,128)(2,1)}), bf16[6144,768]{1,0:T(8,128)(2,1)}) %all-gather.5.cloned.1.call-update) | async-done | bytes 9437200 | tf_op jit(solution)/shard_map/all_gather | solution.py:253
  96.7 2.7 fusion.5
  99.4 1.7 copy-done.13
  101.0 0.9 fusion.7
  102.0 0.2 fusion.29
  102.2 0.9 fusion.1
  103.1 0.9 fusion.3
  104.4 1.0 pad_maximum_fusion.1
  105.4 56.4 %all-gather.7.cloned.1.call-done = bf16[1536,1536]{1,0:T(8,128)(2,1)} async-done(((bf16[48,1536]{1,0:T(8,128)(2,1)}), bf16[1536,1536]{1,0:T(8,128)(2,1)}) %all-gather.7.cloned.1.call-update) | async-done | bytes 4718608 | tf_op jit(solution)/shard_map/all_gather | solution.py:255
  161.9 25.0 %fusion = bf16[256,1536]{1,0:T(8,128)(2,1)} fusion(bf16[1536,1536]{1,0:T(8,128)(2,1)} %all-gather.7.cloned.1.call-done, bf16[288,1536]{1,0:T(8,128)(2,1)} %pad_maximum_fusion.1, f32[1536]{0:T(1024)S(1)} %copy-done.4, f32[1536]{0:T(1024)S(1)} %mul.458, f32[1536]{0:T(1024)S(1)} %mul.455, f32[1536]{0:T(1024)S(1)} %mul.452, f32[1536]{0:T(1024)S(1)} %mul.449, ...), kind=kOutput, calls=%fused_computation.1 | convolution fusion | flops 1248067584 | bytes 30873600 | tf_op jit(solution)/shard_map/dot_general | solution.py:271
  186.9 2.3 reshape.93
  189.4 1.9 copy-done.1
  191.2 80.2 %shard_map.73 = bf16[256,2048]{1,0:T(8,128)(2,1)S(1)} custom-call(bf16[4,2,64,768]{3,2,1,0:T(8,128)(2,1)S(1)} %bitcast.15, bf16[768,2048]{1,0:T(8,128)(2,1)S(1)} %copy-done.1), custom_call_target="tpu_custom_call" | custom-call | tf_op jit(solution)/shard_map/pallas_call | solution.py:213
  271.5 1.0 copy.13
  (64 shorter events, 1.2 us)
Async XLA Ops:
  6.5 1.7 copy-start
  6.5 39.7 %copy-start.2 = (bf16[1,256,1536]{2,1,0:T(8,128)(2,1)S(1)}, bf16[1,256,1536]{2,1,0:T(8,128)(2,1)}, u32[]{:S(2)}) copy-start(bf16[1,256,1536]{2,1,0:T(8,128)(2,1)} %param.7) | copy-start | bytes 2359300
  6.5 11.9 %copy-start.12 = (f32[384]{0:T(512)S(1)}, f32[384]{0:T(512)}, u32[]{:S(2)}) copy-start(f32[384]{0:T(512)} %param.11) | copy-start | bytes 4612
  6.5 11.9 %copy-start.3 = (f32[31,384]{1,0:T(8,128)S(1)}, f32[31,384]{1,0:T(8,128)}, u32[]{:S(2)}) copy-start(f32[31,384]{1,0:T(8,128)} %param.9) | copy-start | bytes 142852
  6.5 90.1 %all-gather.5.cloned.1.call-start = ((), (), s32[]{:S(2)}) async-start(), calls=%async_computation | async-start | bytes 9732096 | tf_op jit(solution)/shard_map/all_gather | solution.py:253
  9.0 152.8 %all-gather.7.cloned.1.call-start = ((), (), s32[]{:S(2)}) async-start(), calls=%async_computation.1 | async-start | bytes 4866048 | tf_op jit(solution)/shard_map/all_gather | solution.py:255
  11.5 34.8 %collective-permute-start = (bf16[16,1536]{1,0:T(8,128)(2,1)S(1)}, bf16[16,1536]{1,0:T(8,128)(2,1)S(1)}, u32[]{:S(2)}, u32[]{:S(2)}) collective-permute-start(bf16[16,1536]{1,0:T(8,128)(2,1)S(1)} %get-tuple-element.38), channel_id=1, source_target_pairs={{0,1},{1,2},{2,3},{3,4},{4,5},{5,6},{6,7},{8,9},{9,10},{10,11},{11... | collective-permute-start | bytes 147464 | tf_op jit(solution)/shard_map/ppermute | solution.py:247
  16.4 29.8 %collective-permute-start.1 = (bf16[16,1536]{1,0:T(8,128)(2,1)S(1)}, bf16[16,1536]{1,0:T(8,128)(2,1)S(1)}, u32[]{:S(2)}, u32[]{:S(2)}) collective-permute-start(bf16[16,1536]{1,0:T(8,128)(2,1)S(1)} %get-tuple-element.39), channel_id=1, source_target_pairs={{1,0},{2,1},{3,2},{4,3},{5,4},{6,5},{7,6},{9,8},{10,9},{11,10},{12... | collective-permute-start | bytes 147464 | tf_op jit(solution)/shard_map/ppermute | solution.py:248
  96.7 4.4 %copy-start.13 = (bf16[6144,768]{1,0:T(8,128)(2,1)S(1)}, bf16[6144,768]{1,0:T(8,128)(2,1)}, u32[]{:S(2)}) copy-start(bf16[6144,768]{1,0:T(8,128)(2,1)} %all-gather.5.cloned.1.call-done) | copy-start | bytes 28311556
  104.1 57.8 %copy-start.4 = (f32[1536]{0:T(1024)S(1)}, f32[1536]{0:T(1024)}, u32[]{:S(2)}) copy-start(f32[1536]{0:T(1024)} %add.177) | copy-start | bytes 18436
  104.1 57.8 %copy-start.5 = (f32[1536]{0:T(1024)S(1)}, f32[1536]{0:T(1024)}, u32[]{:S(2)}) copy-start(f32[1536]{0:T(1024)} %mul.365) | copy-start | bytes 18436
  104.1 57.8 %copy-start.6 = (f32[1536]{0:T(1024)S(1)}, f32[1536]{0:T(1024)}, u32[]{:S(2)}) copy-start(f32[1536]{0:T(1024)} %mul.410) | copy-start | bytes 18436
  104.1 57.8 %copy-start.7 = (f32[1536]{0:T(1024)S(1)}, f32[1536]{0:T(1024)}, u32[]{:S(2)}) copy-start(f32[1536]{0:T(1024)} %mul.413) | copy-start | bytes 18436
  104.1 57.7 %copy-start.8 = (f32[1536]{0:T(1024)S(1)}, f32[1536]{0:T(1024)}, u32[]{:S(2)}) copy-start(f32[1536]{0:T(1024)} %mul.416) | copy-start | bytes 18436
  104.1 57.7 %copy-start.9 = (f32[1536]{0:T(1024)S(1)}, f32[1536]{0:T(1024)}, u32[]{:S(2)}) copy-start(f32[1536]{0:T(1024)} %mul.419) | copy-start | bytes 18436
  104.1 57.7 %copy-start.10 = (f32[1536]{0:T(1024)S(1)}, f32[1536]{0:T(1024)}, u32[]{:S(2)}) copy-start(f32[1536]{0:T(1024)} %mul.422) | copy-start | bytes 18436
  104.1 57.7 %copy-start.11 = (f32[1536]{0:T(1024)S(1)}, f32[1536]{0:T(1024)}, u32[]{:S(2)}) copy-start(f32[1536]{0:T(1024)} %mul.425) | copy-start | bytes 18436
  189.3 1.9 copy-start.1
Sparse Core Ops, SparseCore 0:
  10.3 86.3 all-gather.4
  99.6 62.2 all-gather.6

commit v3 on v2

--- a/solution.py
+++ b/solution.py
@@ -229,6 +229,168 @@
     )(enc, weight)
 
 
+def gather_kernel(
+    axes, piece_ref, out_ref, own_sem, right_send, left_send, plane_send, core_send, recv
+):
+    sections, seqs, depth = axes
+    section, seq, layer = lax.axis_index("section"), lax.axis_index("seq"), lax.axis_index("tp")
+    core = section % 2
+    me = section * seqs + seq
+    steps = [(2 * i, j) for i in range(sections // 2) for j in range(seqs)][:0:-1]
+
+    barrier = pltpu.get_barrier_semaphore()
+    for i in range(sections):
+        for j in range(seqs):
+            if i + j > 0:
+                pl.semaphore_signal(
+                    barrier, inc=1, device_id_type=MESH,
+                    device_id=((section + i) % sections, (seq + j) % seqs, layer),
+                )
+
+    @pl.when(layer > 0)
+    def _():
+        pl.semaphore_signal(
+            barrier, inc=1, device_id=(section, seq, layer - 1), device_id_type=MESH
+        )
+
+    @pl.when(layer < depth - 1)
+    def _():
+        pl.semaphore_signal(
+            barrier, inc=1, device_id=(section, seq, layer + 1), device_id_type=MESH
+        )
+
+    neighbours = (layer + depth - 1) // depth + (2 * depth - 2 - layer) // depth
+    pl.semaphore_wait(barrier, sections * seqs - 1 + neighbours)
+
+    def send(origin, rank, sem, target):
+        return pltpu.make_async_remote_copy(
+            src_ref=out_ref.at[origin, rank], dst_ref=out_ref.at[origin, rank],
+            send_sem=sem, recv_sem=recv.at[origin, rank],
+            device_id=target, device_id_type=MESH,
+        )
+
+    def right(origin):
+        return send(origin, me, right_send.at[origin], (section, seq, layer + 1))
+
+    def left(origin):
+        return send(origin, me, left_send.at[origin], (section, seq, layer - 1))
+
+    def plane(origin, k):
+        i, j = steps[k]
+        target = ((section + i) % sections, (seq + j) % seqs, layer)
+        return send(origin, me, plane_send.at[origin, k], target)
+
+    def across(origin, rank):
+        return send(
+            origin, rank, core_send.at[origin, rank], (section + 1 - 2 * core, seq, layer)
+        )
+
+    def spread(origin):
+        for k in range(len(steps)):
+            plane(origin, k).start()
+        across(origin, me).start()
+
+    def peer(k):
+        i, j = steps[k]
+        return (section + i) % sections * seqs + (seq + j) % seqs
+
+    own = pltpu.make_async_copy(piece_ref, out_ref.at[layer, me], own_sem)
+    own.start()
+    own.wait()
+
+    @pl.when(layer < depth - 1)
+    def _():
+        right(layer).start()
+
+    @pl.when(layer > 0)
+    def _():
+        left(layer).start()
+
+    spread(layer)
+
+    def relay(origin):
+        for k in range(len(steps)):
+            across(origin, peer(k)).wait_recv()
+            across(origin, peer(k)).start()
+
+    for hop in range(1, depth):
+
+        @pl.when(layer - hop >= 0)
+        def _():
+            across(layer - hop, me).wait_recv()
+
+            @pl.when(layer < depth - 1)
+            def _():
+                right(layer - hop).start()
+
+            spread(layer - hop)
+
+        @pl.when(layer + hop < depth)
+        def _():
+            across(layer + hop, me).wait_recv()
+
+            @pl.when(layer > 0)
+            def _():
+                left(layer + hop).start()
+
+            spread(layer + hop)
+
+        if hop == 1:
+            relay(layer)
+        else:
+
+            @pl.when(layer - hop + 1 >= 0)
+            def _():
+                relay(layer - hop + 1)
+
+            @pl.when(layer + hop - 1 < depth)
+            def _():
+                relay(layer + hop - 1)
+
+    @pl.when(layer - depth + 1 >= 0)
+    def _():
+        relay(layer - depth + 1)
+
+    @pl.when(layer + depth - 1 < depth)
+    def _():
+        relay(layer + depth - 1)
+
+    for origin in range(depth):
+
+        @pl.when((layer < depth - 1) & (origin <= layer))
+        def _():
+            right(origin).wait_send()
+
+        @pl.when((layer > 0) & (origin >= layer))
+        def _():
+            left(origin).wait_send()
+
+        for k in range(len(steps)):
+            plane(origin, k).wait_send()
+        for i in range(0, sections, 2):
+            for j in range(seqs):
+                across(origin, (i + core) * seqs + j).wait_send()
+                across(origin, (i + 1 - core) * seqs + j).wait_recv()
+
+
+def gathered_everywhere(piece):
+    axes = (lax.axis_size("section"), lax.axis_size("seq"), lax.axis_size("tp"))
+    sections, seqs, depth = axes
+    copies = sections * seqs
+    dma = pltpu.SemaphoreType.DMA
+    return pl.pallas_call(
+        functools.partial(gather_kernel, axes),
+        out_shape=jax.ShapeDtypeStruct((depth, copies) + piece.shape, piece.dtype),
+        in_specs=[pl.BlockSpec(memory_space=pl.ANY)],
+        out_specs=pl.BlockSpec(memory_space=pl.ANY),
+        scratch_shapes=[
+            dma, dma((depth,)), dma((depth,)), dma((depth, copies // 2 - 1)),
+            dma((depth, copies)), dma((depth, copies)),
+        ],
+        compiler_params=pltpu.CompilerParams(collective_id=1, has_side_effects=True),
+    )(piece)
+
+
 def per_device(
     frames, pointwise_in, depth_kernel, norm_scale, norm_shift, pointwise_out, adapter_weight
 ):
@@ -250,9 +412,12 @@
     small = jnp.concatenate([depth_kernel, norm_scale[None], norm_shift[None]], axis=0)
     small = lax.all_gather(small, "tp", axis=0)
     small = jnp.swapaxes(small, 0, 1).reshape(taps + 2, channels)
-    win = lax.all_gather(own_piece(pointwise_in, copies, copy_index), everywhere, axis=0, tiled=True)
-    win = win.reshape(tp, channels, 2 * block)
-    wout = lax.all_gather(own_piece(pointwise_out, copies, copy_index), everywhere, axis=0, tiled=True)
+    first_piece = own_piece(pointwise_in, copies, copy_index)
+    second_piece = own_piece(pointwise_out.reshape(-1, 2 * block), copies, copy_index)
+    cut = first_piece.shape[0]
+    weights = gathered_everywhere(jnp.concatenate([first_piece, second_piece], axis=0))
+    win = weights[:, :, :cut].reshape(tp, channels, 2 * block)
+    wout = weights[:, :, cut:].reshape(channels, channels)
 
     extended = jnp.concatenate([before, own, after], axis=0).astype(jnp.float32)
     normed = layer_norm_rows(extended)

time: 280 us -> 252 us (0.900)
  waiting for transfers between devices: 106 us -> 0.01 us
  Pallas kernels: 80.2 us -> 178 us
  matrix products: 30.5 us -> 16.9 us
  between operations: 13.7 us -> 0.4 us
  local copies, waits for them, and re-layouts: 23.5 us -> 30.4 us
    all_gather x2 -> x0, waiting for transfers between devices: 106 us -> none  [the longest x1 56.4 us: per_device(): lax.all_gather(own_piece(pointwise_out, copies, copy_index), everywhere,...]
    pallas_call x0 -> x1, Pallas kernels: none -> 101 us  [gathered_everywhere(): pl.pallas_call(functools.partial(gather_kernel, axes), out_shape=jax.Shap...]
    dot_general x1, matrix products: 25 us -> 8.38 us  [per_device(): mixed = jnp.dot(activated, wout, preferred_element_type=jnp.float32)]
    slice x0 -> x2, local copies, waits for them, and re-layouts: none -> 11.7 us  [the longest x1 6.9 us: per_device(): projected = jnp.dot(normed, win[b], preferred_element_type=jnp.float32)]
    reshape x0 -> x2, local copies, waits for them, and re-layouts: none -> 10.2 us  [the longest x1 8.03 us: per_device(): wout = weights[:, :, cut:].reshape(channels, channels)]
    mul x31, local copies, waits for them, and re-layouts: 8.57 us -> 0.27 us  [per_device(): padded[first + offset:first + offset + rows] * small[offset]]
    pallas_call x1, Pallas kernels: 80.2 us -> 76.9 us  [adapter(): pl.pallas_call(functools.partial(adapter_kernel, axes, tile), out_shape=j...]
    unnamed x29 -> x23, local copies, waits for them, and re-layouts: 6.22 us -> 2.97 us
  transfers between devices with their start and end apart: 4 -> 2, of which waited for: 2 -> 0; matrix products, arithmetic and copies ran while one was open for 8% -> 10% of each run, Pallas kernels for 0% -> 40%
where the time goes in v3:
time: 252 us; the launch traced here: 251 us
  Pallas kernels  178 us (71%)
  local copies, waits for them, and re-layouts  30.4 us (12%)
  matrix products  16.9 us (7%)
  blocking collectives  13.9 us (6%)
  starting transfers between devices  6.81 us (3%)
  other arithmetic  4.54 us (2%)
    pallas_call x1, Pallas kernels, gathered_everywhere(): pl.pallas_call(functools.partial(gather_kernel, axes), out_shape=jax.Shap...  101 us
    pallas_call x1, Pallas kernels, adapter(): pl.pallas_call(functools.partial(adapter_kernel, axes, tile), out_shape=j...  76.9 us
    all_gather x1, blocking collectives, per_device(): small = lax.all_gather(small, 'tp', axis=0)  13.9 us
    dot_general x4, matrix products, per_device(): projected = jnp.dot(normed, win[b], preferred_element_type=jnp.float32)  8.5 us
    dot_general x1, matrix products, per_device(): mixed = jnp.dot(activated, wout, preferred_element_type=jnp.float32)  8.38 us
    reshape x1, local copies, waits for them, and re-layouts, per_device(): wout = weights[:, :, cut:].reshape(channels, channels)  8.03 us
    slice x1, local copies, waits for them, and re-layouts, per_device(): projected = jnp.dot(normed, win[b], preferred_element_type=jnp.float32)  6.9 us
    ppermute x1, starting transfers between devices, per_device(): lax.ppermute(own[rows - HALO:], ('seq', 'tp'), [(i, i + 1) for i in range...  5.53 us
  transfers between devices with their start and end apart: 2, of which 0 were waited for; matrix products, arithmetic and copies ran while one was open for 10% of the time, Pallas kernels for 40%

profile of v3, /device:TPU:0, one launch (start us, length us, event | category | flops | bytes accessed | tf_op | source)
XLA Modules:
  0.0 251.1 jit_solution(5574364673364884270)
XLA Ops:
  0.0 1.6 slice_bitcast_fusion.1
  1.6 5.5 %collective-permute-start = (bf16[16,1536]{1,0:T(8,128)(2,1)}, bf16[16,1536]{1,0:T(8,128)(2,1)}, u32[]{:S(2)}, u32[]{:S(2)}) collective-permute-start(bf16[16,1536]{1,0:T(8,128)(2,1)} %get-tuple-element.42), channel_id=1, source_target_pairs={{0,1},{1,2},{2,3},{3,4},{4,5},{5,6},{6,7},{8,9},{9,10},{10,11},{11... | collective-permute-start | bytes 147464 | tf_op jit(solution)/shard_map/ppermute | solution.py:409
  7.1 1.3 collective-permute-start.1
  8.4 2.2 reshape.99
  10.6 0.7 constant_dynamic-slice_fusion
  11.3 1.7 pad_maximum_fusion.2.piece_ref
  13.0 101.2 %shard_map.73 = bf16[4,8,288,768]{3,2,1,0:T(8,128)(2,1)} custom-call(bf16[288,768]{1,0:T(8,128)(2,1)} %pad_maximum_fusion.2.piece_ref), custom_call_target="tpu_custom_call" | custom-call | tf_op jit(solution)/shard_map/pallas_call | solution.py:381
  114.3 0.0 copy-start.7
  114.3 0.0 copy-start.8
  114.3 0.0 copy-start.6
  114.3 6.9 %fusion.34 = (bf16[1,8,192,768]{3,2,1,0:T(8,128)(2,1)}, bf16[1,8,192,768]{3,2,1,0:T(8,128)(2,1)}, bf16[1,8,192,768]{3,2,1,0:T(8,128)(2,1)}, bf16[1,8,192,768]{3,2,1,0:T(8,128)(2,1)}) fusion(bf16[4,8,288,768]{3,2,1,0:T(8,128)(2,1)} %shard_map.73), kind=kLoop, calls=%fused_computation.82 | loop fusion | bytes 18874368 | tf_op jit(solution)/shard_map/slice | solution.py:426
  121.2 13.9 %all-gather.1 = f32[4,33,384]{2,1,0:T(8,128)S(1)} all-gather(f32[1,33,384]{2,1,0:T(8,128)S(1)} %maximum_bitcast_fusion), channel_id=2, replica_groups=mesh['section'=4,'seq'=2,'tp'=4] {'tp'}, dimensions={0}, use_global_device_ids=true | all-gather | bytes 253440 | tf_op jit(solution)/shard_map/all_gather | solution.py:413
  135.2 0.3 slice_reduce_fusion.32
  135.5 0.2 slice_reduce_fusion.31
  135.8 4.8 %slice.365 = bf16[4,8,96,768]{3,2,1,0:T(8,128)(2,1)} slice(bf16[4,8,288,768]{3,2,1,0:T(8,128)(2,1)} %shard_map.73), slice={[0:4], [0:8], [192:288], [0:768]} | slice | bytes 9437184 | tf_op jit(solution)/shard_map/slice | solution.py:420
  140.5 8.0 %reshape.100 = bf16[1536,1536]{1,0:T(8,128)(2,1)} reshape(bf16[4,8,96,768]{3,2,1,0:T(8,128)(2,1)} %slice.365) | data formatting | bytes 9437184 | tf_op jit(solution)/shard_map/reshape | solution.py:420
  149.0 1.0 convert_reduce_fusion
  150.1 1.2 fusion.3
  151.3 2.8 %fusion.30 = f32[288,768]{1,0:T(8,128)S(1)} fusion(bf16[1536,768]{1,0:T(8,128)(2,1)} %bitcast.37, f32[288]{0:T(512)S(1)} %add_rsqrt_fusion, f32[288]{0:T(512)S(1)} %broadcast_multiply_fusion, bf16[16,1536]{1,0:T(8,128)(2,1)} %collective-permute-done.1, bf16[256,1536]{1,0:T(8,128)(2,1)S(1)} %bitcast.30, bf16[16,1536]{1,0:T(8,128)(2,1)} %collective-permute-done), kind=kOutput, calls=%fused_computation.80 | convolution fusion | flops 683458560 | bytes 4131072 | tf_op jit(solution)/shard_map/dot_general | solution.py:426
  154.1 1.9 fusion.32
  156.0 0.2 fusion.21
  156.3 1.9 fusion.26
  158.2 1.9 fusion.28
  160.1 0.2 fusion.23
  160.4 0.1 pad_maximum_fusion.1
  160.5 0.1 slice-done.1
  160.5 8.4 %fusion = bf16[256,1536]{1,0:T(8,128)(2,1)} fusion(bf16[1536,1536]{1,0:T(8,128)(2,1)S(1)} %bitcast.27, bf16[288,1536]{1,0:T(8,128)(2,1)S(1)} %pad_maximum_fusion.1, f32[1536]{0:T(1024)S(1)} %add.178, f32[1536]{0:T(1024)S(1)} %mul.459, f32[1536]{0:T(1024)S(1)} %mul.456, f32[1536]{0:T(1024)S(1)} %mul.453, f32[1536]{0:T(1024)S(1)} %mul.450, ...), kind=kOutput, calls=%fused_computation.1 | convolution fusion | flops 1248067584 | bytes 30941184 | tf_op jit(solution)/shard_map/dot_general | solution.py:436
  168.9 2.3 reshape.101
  171.2 0.1 copy.11
  171.3 1.9 copy-done.1
  173.2 76.9 %shard_map.74 = bf16[256,2048]{1,0:T(8,128)(2,1)S(1)} custom-call(bf16[4,2,64,768]{3,2,1,0:T(8,128)(2,1)S(1)} %bitcast.25, bf16[768,2048]{1,0:T(8,128)(2,1)S(1)} %copy-done.1), custom_call_target="tpu_custom_call" | custom-call | tf_op jit(solution)/shard_map/pallas_call | solution.py:213
  250.2 1.0 copy.13
  (59 shorter events, 0.4 us)
Async XLA Ops:
  0.0 11.3 %copy-start = (bf16[1536,768]{1,0:T(8,128)(2,1)S(1)}, bf16[1536,768]{1,0:T(8,128)(2,1)}, u32[]{:S(2)}) copy-start(bf16[1536,768]{1,0:T(8,128)(2,1)} %param.8) | copy-start | bytes 7077892
  1.6 147.4 %collective-permute-start = (bf16[16,1536]{1,0:T(8,128)(2,1)}, bf16[16,1536]{1,0:T(8,128)(2,1)}, u32[]{:S(2)}, u32[]{:S(2)}) collective-permute-start(bf16[16,1536]{1,0:T(8,128)(2,1)} %get-tuple-element.42), channel_id=1, source_target_pairs={{0,1},{1,2},{2,3},{3,4},{4,5},{5,6},{6,7},{8,9},{9,10},{10,11},{11... | collective-permute-start | bytes 147464 | tf_op jit(solution)/shard_map/ppermute | solution.py:409
  7.1 141.8 %collective-permute-start.1 = (bf16[16,1536]{1,0:T(8,128)(2,1)}, bf16[16,1536]{1,0:T(8,128)(2,1)}, u32[]{:S(2)}, u32[]{:S(2)}) collective-permute-start(bf16[16,1536]{1,0:T(8,128)(2,1)} %get-tuple-element.43), channel_id=1, source_target_pairs={{1,0},{2,1},{3,2},{4,3},{5,4},{6,5},{7,6},{9,8},{10,9},{11,10},{12... | collective-permute-start | bytes 147464 | tf_op jit(solution)/shard_map/ppermute | solution.py:410
  114.3 6.9 %copy-start.7 = (f32[384]{0:T(512)S(1)}, f32[384]{0:T(512)}, u32[]{:S(2)}) copy-start(f32[384]{0:T(512)} %param.10) | copy-start | bytes 4612
  114.3 6.9 %copy-start.8 = (f32[384]{0:T(512)S(1)}, f32[384]{0:T(512)}, u32[]{:S(2)}) copy-start(f32[384]{0:T(512)} %param.11) | copy-start | bytes 4612
  114.3 6.9 %copy-start.6 = (f32[31,384]{1,0:T(8,128)S(1)}, f32[31,384]{1,0:T(8,128)}, u32[]{:S(2)}) copy-start(f32[31,384]{1,0:T(8,128)} %param.9) | copy-start | bytes 142852
  140.5 8.5 %copy-start.2 = (bf16[1,256,1536]{2,1,0:T(8,128)(2,1)S(1)}, bf16[1,256,1536]{2,1,0:T(8,128)(2,1)}, u32[]{:S(2)}) copy-start(bf16[1,256,1536]{2,1,0:T(8,128)(2,1)} %param.7) | copy-start | bytes 2359300
  151.3 2.8 %copy-start.5 = (bf16[1,8,192,768]{3,2,1,0:T(8,128)(2,1)S(1)}, bf16[1,8,192,768]{3,2,1,0:T(8,128)(2,1)}, u32[]{:S(2)}) copy-start(bf16[1,8,192,768]{3,2,1,0:T(8,128)(2,1)} %get-tuple-element.38) | copy-start | bytes 7077892
  154.1 2.2 copy-start.4
  156.3 1.9 copy-start.3
  158.2 2.3 slice-start
  158.2 2.3 slice-start.1
  171.3 1.9 copy-start.1
